TPU v7x, 32 devices: a whole 2x2x4 slice. The times are simulated.
32 devices in a mesh: groups: 2 (over y), fsdp: 4 (over z), tenant: 2 (over x), pair: 2 (over core).
Axes of the slice: x: 2, y: 2, z: 4, core: 2. Of those that a mesh axis runs over, the one named last changes fastest.
Arguments:
- hidden: bfloat16 [2, 32, 128, 8192], P('pair', ('groups', 'fsdp', 'tenant')), parts along dimension 1, may hold values from -6 to 6
- pair_adapter_index: int32 [32], P(('groups', 'fsdp', 'tenant')), parts along dimension 0, may hold values from 0 to 3
- live_block_count: int32 [16], P(('groups', 'fsdp', 'tenant')), parts along dimension 0, may hold values from 0 to 2, as said below
- lengths: int32 [2, 32], P('pair', ('groups', 'fsdp', 'tenant')), parts along dimension 1, may hold values from 1 to 128, as said below
- adapter_storage_row: int32 [4], replicated, may hold values from 0 to 3, each once
- frozen_base_weight: bfloat16 [8192, 512], P(('fsdp', 'pair')), may hold values from -0.0625 to 0.0625
- adapter_down_maps: bfloat16 [4, 8192, 64], P('tenant', ('fsdp', 'pair')), may hold values from -0.0625 to 0.0625
- adapter_up_maps: bfloat16 [4, 512, 64], P('tenant', ('fsdp', 'pair')), may hold values from -0.75 to 0.75
- readout: float32 [512], replicated, may hold values from -6 to 6
- reference_score_margin: float32 [32], P(('groups', 'fsdp', 'tenant')), parts along dimension 0, may hold values from -600 to 600
Outputs:
- pair_loss: float32 [32], P(('groups', 'fsdp', 'tenant')), parts along dimension 0
- down_gradient: bfloat16 [8, 8192, 64], P(('groups', 'tenant'), ('fsdp', 'pair')), parts along dimension 0
- up_gradient: bfloat16 [8, 512, 64], P(('groups', 'tenant'), ('fsdp', 'pair')), parts along dimension 0
There are 2 independent parts, one for each index of `groups`. A program takes and returns all parts, laid end to end along the dimension named above; an argument that names none is the same for every part. Nothing has to cross between parts.
Inputs may be any that keep to these rules, and one draw needn't show every extreme that they name: A holder's first live_block_count slots hold live pairs, the rest are padding. A block's first lengths positions are live. `adapter_storage_row`: each storage row once.
All inputs are finite; a program needn't handle non-finite values.
Results may differ from a plain program's by a relative error of at most 0.0068.
Values may be sent and summed in bfloat16 or wider, within the bound.
A program may use at most 64 MiB of HBM per device.

v0:
```python
import jax
import jax.numpy as jnp
from jax import lax
from jax.sharding import PartitionSpec as P

beta_value = 0.01


def shards(
    hidden,
    pair_adapter_index,
    live_block_count,
    lengths,
    adapter_storage_row,
    frozen_base_weight,
    adapter_down_maps,
    adapter_up_maps,
    readout,
    reference_score_margin,
):
    tokens = hidden[0]
    slot_count, block_rows, feature_count = tokens.shape
    token_rows = slot_count * block_rows
    flat_tokens = tokens.reshape(token_rows, feature_count)
    out_count = frozen_base_weight.shape[1]
    adapter_count = adapter_storage_row.shape[0]
    rank_length = adapter_down_maps.shape[2]
    parity = lax.axis_index("pair")
    pair_count = lax.axis_size("pair")
    fsdp_count = lax.axis_size("fsdp")
    catalog = jnp.arange(adapter_count, dtype=jnp.int32)
    adapter_slot = jnp.sum(
        jnp.where(pair_adapter_index[:, None] == catalog[None, :], adapter_storage_row[None, :], 0),
        axis=1,
    )
    all_down, all_up = (
        lax.all_gather(adapter_down_maps, "tenant", axis=0, tiled=True),
        lax.all_gather(adapter_up_maps, "tenant", axis=0, tiled=True),
    )
    fsdp_slots = lax.all_gather(adapter_slot, "fsdp", axis=0, tiled=True)
    peer_slots = jnp.broadcast_to(
        fsdp_slots.reshape(fsdp_count, 1, slot_count), (fsdp_count, pair_count, slot_count)
    ).reshape(-1)
    selector = (peer_slots[:, None] == catalog[None, :]).astype(jnp.bfloat16)
    peer_total = peer_slots.shape[0]
    chosen_down = jnp.dot(
        selector, all_down.reshape(adapter_count, -1), preferred_element_type=jnp.float32
    )
    chosen_down = chosen_down.astype(jnp.bfloat16).reshape(peer_total, -1, rank_length)
    chosen_up = jnp.dot(
        selector, all_up.reshape(adapter_count, -1), preferred_element_type=jnp.float32
    )
    chosen_up = chosen_up.astype(jnp.bfloat16).reshape(peer_total, -1, rank_length)
    full_down, full_up = (
        lax.all_to_all(chosen_down, ("fsdp", "pair"), split_axis=0, concat_axis=1, tiled=True),
        lax.all_to_all(chosen_up, ("fsdp", "pair"), split_axis=0, concat_axis=1, tiled=True),
    )
    base_part = jnp.dot(
        flat_tokens,
        lax.all_gather(frozen_base_weight, ("fsdp", "pair"), axis=0, tiled=True),
        preferred_element_type=jnp.float32,
    )
    low_rank = jnp.einsum(
        "btd,bdr->btr", tokens, full_down, preferred_element_type=jnp.float32
    ).astype(jnp.bfloat16)
    adapted = jnp.einsum("btr,bor->bto", low_rank, full_up, preferred_element_type=jnp.float32)
    mixed_out = base_part.reshape(slot_count, block_rows, out_count) + adapted
    gate_value = jax.nn.sigmoid(mixed_out)
    token_score = jnp.einsum(
        "bto,o->bt", mixed_out * gate_value, readout, precision=lax.Precision.HIGHEST
    )
    position = jnp.arange(block_rows, dtype=jnp.int32)
    valid_mask = (position[None, :] < lengths[0][:, None]).astype(jnp.float32)
    seq_score = jnp.sum(valid_mask * token_score, axis=1)
    half_sign = 1.0 - 2.0 * parity.astype(jnp.float32)
    margin = lax.psum(half_sign * seq_score, "pair")
    pair_logit = beta_value * (margin - reference_score_margin)
    alive_mask = (jnp.arange(slot_count, dtype=jnp.int32) < live_block_count[0]).astype(jnp.float32)
    pair_loss = alive_mask * jax.nn.softplus(-pair_logit)
    factor = -beta_value * jax.nn.sigmoid(-pair_logit) * alive_mask * half_sign
    slope = gate_value * (1.0 + mixed_out * (1.0 - gate_value))
    cotangent = (factor[:, None, None] * valid_mask[:, :, None] * readout * slope).astype(
        jnp.bfloat16
    )
    up_rows = jnp.einsum("bto,btr->bor", cotangent, low_rank, preferred_element_type=jnp.float32)
    low_grad = jnp.einsum(
        "bto,bor->btr", cotangent, full_up, preferred_element_type=jnp.float32
    ).astype(jnp.bfloat16)
    down_rows = jnp.einsum("btd,btr->bdr", tokens, low_grad, preferred_element_type=jnp.float32)
    got_down, got_up = (
        lax.all_to_all(down_rows, ("fsdp", "pair"), split_axis=1, concat_axis=0, tiled=True),
        lax.all_to_all(up_rows, ("fsdp", "pair"), split_axis=1, concat_axis=0, tiled=True),
    )
    source_count = peer_slots.shape[0]
    routing = (catalog[:, None] == peer_slots[None, :]).astype(jnp.float32)
    term_down = jnp.dot(
        routing,
        got_down.reshape(source_count, -1),
        precision=lax.Precision.HIGHEST,
        preferred_element_type=jnp.float32,
    )
    term_up = jnp.dot(
        routing,
        got_up.reshape(source_count, -1),
        precision=lax.Precision.HIGHEST,
        preferred_element_type=jnp.float32,
    )
    holder_down_map, holder_up_map = (
        lax.psum_scatter(term_down, "tenant", scatter_dimension=0, tiled=True),
        lax.psum_scatter(term_up, "tenant", scatter_dimension=0, tiled=True),
    )
    down_gradient = holder_down_map.reshape(adapter_down_maps.shape).astype(jnp.bfloat16)
    up_gradient = holder_up_map.reshape(adapter_up_maps.shape).astype(jnp.bfloat16)
    return (pair_loss, down_gradient, up_gradient)


def solution(mesh):
    return jax.shard_map(
        shards,
        mesh=mesh,
        in_specs=(
            P("pair", ("groups", "fsdp", "tenant"), None, None),
            P(("groups", "fsdp", "tenant")),
            P(("groups", "fsdp", "tenant")),
            P("pair", ("groups", "fsdp", "tenant")),
            P(),
            P(("fsdp", "pair"), None),
            P("tenant", ("fsdp", "pair"), None),
            P("tenant", ("fsdp", "pair"), None),
            P(),
            P(("groups", "fsdp", "tenant")),
        ),
        out_specs=(
            P(("groups", "fsdp", "tenant")),
            P(("groups", "tenant"), ("fsdp", "pair"), None),
            P(("groups", "tenant"), ("fsdp", "pair"), None),
        ),
        check_vma=False,
    )
```

profile of v0, /device:TPU:0, one launch (start us, length us, event | category | flops | bytes accessed | tf_op | source)
XLA Modules:
  0.0 375.3 jit_solution(11623130162755755926)
XLA Ops:
  7.9 1.2 dynamic-slice
  9.8 0.9 fusion.16
  10.9 9.9 %all-reduce = s32[8]{0:T(128)S(1)} all-reduce(s32[8]{0:T(128)S(1)} %dynamic-update-slice), channel_id=1, replica_groups=mesh['groups'=2,'fsdp'=4,'tenant'=2,'pair'=2] {'fsdp'}, use_global_device_ids=true, to_apply=%add | all-reduce | flops 8 | bytes 64
  21.0 4.8 %all_gather.15 = bf16[4,64,64]{2,1,0:T(8,128)(2,1)S(1)} all-gather(bf16[2,64,64]{2,1,0:T(8,128)(2,1)} %param.17), channel_id=1, replica_groups=mesh['groups'=2,'fsdp'=4,'tenant'=2,'pair'=2] {'tenant'}, dimensions={0}, use_global_device_ids=true | all-gather | bytes 49152 | tf_op jit(solution)/shard_map/all_gather | solution.py:38
  26.4 0.9 reshape.99
  27.3 3.4 all-to-all-start.1
  30.6 9.5 %all_gather.14 = bf16[4,1024,64]{1,2,0:T(8,128)(2,1)S(1)} all-gather(bf16[2,1024,64]{1,2,0:T(8,128)(2,1)} %param.16), channel_id=1, replica_groups=mesh['groups'=2,'fsdp'=4,'tenant'=2,'pair'=2] {'tenant'}, dimensions={0}, use_global_device_ids=true | all-gather | bytes 786432 | tf_op jit(solution)/shard_map/all_gather | solution.py:37
  41.3 0.8 convolution_convert_fusion
  42.1 5.8 %reshape.84 = bf16[16,1024,64]{2,1,0:T(8,128)(2,1)} reshape(bf16[16,65536]{1,0:T(8,128)(2,1)S(1)} %convolution_convert_fusion) | data formatting | bytes 4194304 | tf_op jit(solution)/shard_map/reshape | solution.py:49
  47.8 4.8 %copy.32 = bf16[16,1024,64]{1,2,0:T(8,128)(2,1)} copy(bf16[16,1024,64]{2,1,0:T(8,128)(2,1)} %reshape.84) | data formatting | bytes 4194304 | tf_op jit(solution)/shard_map/reshape | solution.py:49
  52.6 4.8 %all-to-all-start = ((bf16[16,1024,64]{1,2,0:T(8,128)(2,1)}), bf16[16,1024,64]{1,2,0:T(8,128)(2,1)S(1)}, u32[]{:S(2)}, u32[]{:S(2)}) async-start(bf16[16,1024,64]{1,2,0:T(8,128)(2,1)} %copy.32), calls=%async_computation | async-start | bytes 4194304 | tf_op jit(solution)/shard_map/all_to_all | solution.py:55
  58.0 82.3 %all-to-all-done = bf16[16,1024,64]{1,2,0:T(8,128)(2,1)S(1)} async-done(((bf16[16,1024,64]{1,2,0:T(8,128)(2,1)}), bf16[16,1024,64]{1,2,0:T(8,128)(2,1)S(1)}, u32[]{:S(2)}, u32[]{:S(2)}) %all-to-all-start) | async-done | bytes 2097184 | tf_op jit(solution)/shard_map/all_to_all | solution.py:55
  140.3 2.5 copy.45
  142.8 2.9 all_to_all.51
  145.7 3.8 fusion.6
  149.5 7.0 %fusion = f32[2,128,512]{2,1,0:T(8,128)S(1)} fusion(bf16[8192,512]{1,0:T(8,128)(2,1)} %all-gather.2.cloned.1.call-done, bf16[1,2,128,8192]{3,2,1,0:T(8,128)(2,1)} %param.10), kind=kOutput, calls=%fused_computation.2 | convolution fusion | flops 2147483648 | bytes 13107200 | tf_op jit(solution)/shard_map/dot_general | solution.py:58
  158.3 2.5 psum.7
  162.0 1.3 reshape.103
  163.3 3.6 all-to-all-start.3
  166.9 5.0 %convolution_bitcast_fusion = f32[2,8192,64]{1,2,0:T(8,128)} fusion(bf16[1,2,128,8192]{3,2,1,0:T(8,128)(2,1)} %param.10, bf16[2,128,512]{2,1,0:T(8,128)(2,1)S(1)} %multiply_convert_fusion, bf16[2,512,64]{1,2,0:T(8,128)(2,1)S(1)} %all_to_all.55), kind=kOutput, calls=%fused_computation.1 | convolution fusion | flops 285229056 | bytes 8781824 | tf_op jit(solution)/shard_map/btd,btr->bdr/dot_general | solution.py:89
  171.9 10.8 %copy.35 = f32[2,8192,64]{2,0,1:T(2,128)} copy(f32[2,8192,64]{1,2,0:T(8,128)} %convolution_bitcast_fusion) | data formatting | bytes 8388608 | tf_op jit(solution)/shard_map/btd,btr->bdr/dot_general | solution.py:89
  182.7 12.0 %reshape.101 = f32[8,1,131072]{2,1,0:T(1,128)} reshape(f32[8192,2,64]{2,1,0:T(2,128)} %bitcast.64) | data formatting | bytes 8388608
  194.7 5.0 %all-to-all-start.2 = ((f32[8,1,131072]{2,1,0:T(1,128)}), f32[8,1,131072]{2,1,0:T(1,128)}, u32[]{:S(2)}, u32[]{:S(2)}) async-start(f32[8,1,131072]{2,1,0:T(1,128)} %reshape.101), calls=%async_computation.2 | async-start | bytes 8388608 | tf_op jit(solution)/shard_map/all_to_all | solution.py:91
  201.4 1.3 reduce.1
  203.5 90.2 %all-to-all-done.2 = f32[8,1,131072]{2,1,0:T(1,128)} async-done(((f32[8,1,131072]{2,1,0:T(1,128)}), f32[8,1,131072]{2,1,0:T(1,128)}, u32[]{:S(2)}, u32[]{:S(2)}) %all-to-all-start.2) | async-done | bytes 4194336 | tf_op jit(solution)/shard_map/all_to_all | solution.py:91
  293.8 13.7 %reduce = f32[8,131072]{1,0:T(8,128)} reduce(f32[8,1,131072]{2,1,0:T(1,128)} %all-to-all-done.2, f32[]{:T(128)} %broadcast.73), dimensions={1}, to_apply=%all_to_all.56.reduce_sub_computation | reduce | bytes 8388612 | tf_op jit(solution)/shard_map/all_to_all | solution.py:91
  307.5 11.5 %reshape.102 = f32[8192,2,64]{2,1,0:T(2,128)} reshape(f32[8,131072]{1,0:T(8,128)} %reduce) | data formatting | bytes 8388608
  319.0 7.5 %copy.44 = f32[2,8,1024,64]{3,2,0,1:T(8,128)} copy(f32[2,8,1024,64]{3,0,2,1:T(2,128)} %bitcast.65) | data formatting | bytes 8388608 | tf_op jit(solution)/shard_map/all_to_all | solution.py:91
  326.5 6.0 %reshape.87 = f32[16,65536]{1,0:T(8,128)} reshape(f32[8,2,1024,64]{3,2,1,0:T(8,128)} %bitcast.66) | data formatting | bytes 8388608 | tf_op jit(solution)/shard_map/reshape | solution.py:98
  332.4 3.7 fusion.15
  336.2 30.0 %all-reduce.5 = (bf16[4,65536]{1,0:T(4,128)(2,1)S(1)}, bf16[4,4096]{1,0:T(4,128)(2,1)S(1)}) all-reduce(f32[4,65536]{1,0:T(4,128)S(1)} %fusion.15, f32[4,4096]{1,0:T(4,128)S(1)} %fusion.14), channel_id=2, replica_groups=mesh['groups'=2,'fsdp'=4,'tenant'=2,'pair'=2] {'tenant'}, use_global_device_ids=true, to_apply=%region_3.4.clone | all-reduce | flops 278528 | bytes 1671168
  367.6 0.9 copy.39
  (45 shorter events, 9.1 us)
Async XLA Ops:
  7.2 142.4 %all-gather.2.cloned.1.call-start = ((), (), s32[]{:S(2)}) async-start(), calls=%async_computation.4 | async-start | bytes 9437184 | tf_op jit(solution)/shard_map/all_gather | solution.py:60
  27.3 25.4 %all-to-all-start.1 = ((bf16[8,2,4096]{2,1,0:T(2,128)(2,1)}), bf16[8,2,4096]{2,1,0:T(2,128)(2,1)S(1)}, u32[]{:S(2)}, u32[]{:S(2)}) async-start(bf16[8,2,4096]{2,1,0:T(2,128)(2,1)} %reshape.99), calls=%async_computation.1 | async-start | bytes 262144 | tf_op jit(solution)/shard_map/all_to_all | solution.py:56
  52.6 87.7 %all-to-all-start = ((bf16[16,1024,64]{1,2,0:T(8,128)(2,1)}), bf16[16,1024,64]{1,2,0:T(8,128)(2,1)S(1)}, u32[]{:S(2)}, u32[]{:S(2)}) async-start(bf16[16,1024,64]{1,2,0:T(8,128)(2,1)} %copy.32), calls=%async_computation | async-start | bytes 4194304 | tf_op jit(solution)/shard_map/all_to_all | solution.py:55
  149.5 7.3 %copy-start = (f32[512]{0:T(512)S(1)}, f32[512]{0:T(512)}, u32[]{:S(2)}) copy-start(f32[512]{0:T(512)} %param.18) | copy-start | bytes 6148
  149.5 7.9 %copy-start.1 = (s32[1,2]{1,0:T(1,128)S(1)}, s32[1,2]{1,0:T(1,128)}, u32[]{:S(2)}) copy-start(s32[1,2]{1,0:T(1,128)} %param.13) | copy-start | bytes 28
  149.5 11.2 %copy-start.2 = (f32[2]{0:T(128)S(1)}, f32[2]{0:T(128)}, u32[]{:S(2)}) copy-start(f32[2]{0:T(128)} %param.19) | copy-start | bytes 28
  163.3 31.4 %all-to-all-start.3 = ((f32[8,1,8192]{2,1,0:T(1,128)}), f32[8,1,8192]{2,1,0:T(1,128)S(1)}, u32[]{:S(2)}, u32[]{:S(2)}) async-start(f32[8,1,8192]{2,1,0:T(1,128)} %reshape.103), calls=%async_computation.3 | async-start | bytes 524288 | tf_op jit(solution)/shard_map/all_to_all | solution.py:92
  194.7 5.0 %copy-start.3 = (u32[32]{0:T(128)S(1)}, u32[32]{0:T(128)}, u32[]{:S(2)}) copy-start(u32[32]{0:T(128)} %constant.37) | copy-start | bytes 388
  194.7 99.1 %all-to-all-start.2 = ((f32[8,1,131072]{2,1,0:T(1,128)}), f32[8,1,131072]{2,1,0:T(1,128)}, u32[]{:S(2)}, u32[]{:S(2)}) async-start(f32[8,1,131072]{2,1,0:T(1,128)} %reshape.101), calls=%async_computation.2 | async-start | bytes 8388608 | tf_op jit(solution)/shard_map/all_to_all | solution.py:91
Sparse Core Ops, SparseCore 0:
  9.6 127.2 all-gather.1
where the time goes:
time: 377 us; the launch traced here: 375 us
  waiting for transfers between devices  173 us (46%)
  local copies, waits for them, and re-layouts  73.9 us (20%)
  blocking collectives  56.6 us (15%)
  matrix products  21.7 us (6%)
  starting transfers between devices  16.8 us (4%)
  other arithmetic  16.8 us (4%)
  between operations  16.2 us (4%)
    all_to_all x1, waiting for transfers between devices, shards(): lax.all_to_all(down_rows, ('fsdp', 'pair'), split_axis=1, concat_axis=0,...  90.2 us
    all_to_all x1, waiting for transfers between devices, shards(): lax.all_to_all(chosen_down, ('fsdp', 'pair'), split_axis=0, concat_axis=1...  82.3 us
    unnamed x2, blocking collectives  39.9 us
    unnamed x19, local copies, waits for them, and re-layouts  29.2 us
    all_to_all x1, other arithmetic, shards(): lax.all_to_all(down_rows, ('fsdp', 'pair'), split_axis=1, concat_axis=0,...  13.7 us
    dot_general x1, local copies, waits for them, and re-layouts, shards(): jnp.einsum('btd,btr->bdr', tokens, low_grad, preferred_element_type=jnp.f...  10.8 us
    reshape x2, local copies, waits for them, and re-layouts, shards(): chosen_down.astype(jnp.bfloat16).reshape(peer_total, -1, rank_length)  10.6 us
    all_gather x1, blocking collectives, shards(): lax.all_gather(adapter_down_maps, 'tenant', axis=0, tiled=True)  9.49 us
  transfers between devices with their start and end apart: 5, of which 2 were waited for; matrix products, arithmetic and copies ran while one was open for 14% of the time, Pallas kernels for 0%

commit v1 on v0

v1 whole, which is shorter than its diff:
```python
import jax
import jax.numpy as jnp
from jax import lax
from jax.experimental import pallas as pl
from jax.experimental.pallas import tpu as pltpu
from jax.sharding import PartitionSpec as P

BETA = 0.01
F32, BF16 = jnp.float32, jnp.bfloat16
NN = (((1,), (0,)), ((), ()))
NT = (((1,), (1,)), ((), ()))


def dot(a, b, dims=NN):
    return lax.dot_general(a, b, dims, preferred_element_type=F32)


def step_kernel(
    sizes,
    scalars, readout, marks, hidden, base, down, up,
    loss_out, down_out, up_out,
    tokens, wbuf, dbuf, ubuf, mbuf, acc, lacc, pacc, placc,
    score, pscore, lowm, cot, lgt, upsum, upeer, uz, ur, ps, pr, xs, xr, xus, xur,
    loc, locw, tok_s, tok_r, zw_s, zw_r, zd_s, zd_r, zu_s, zu_r, zm_s, zm_r,
    xw_s, xw_r, xd_s, xd_r, yw_s, yw_r, cu_s, cu_r, xu_s, xu_r,
    part_s, part_r, score_s, score_r, mid_s, mid_r, p_s, p_r, q_s, q_r, xg_s, xg_r,
):
    groups, fsdp, tenant, shares, rank = sizes
    g, f = lax.axis_index("groups"), lax.axis_index("fsdp")
    t, p = lax.axis_index("tenant"), lax.axis_index("pair")
    slots, block = 2, tokens.shape[2] // 2
    width = tokens.shape[3]
    lanes = slots * rank
    quarter = g * shares + lax.rem(t, shares)
    side_t = t + 1 - 2 * lax.rem(t, 2)

    def remote(src, dst, send, recv, **where):
        return pltpu.make_async_remote_copy(
            src_ref=src, dst_ref=dst, send_sem=send, recv_sem=recv,
            device_id=where, device_id_type=pl.DeviceIdType.MESH,
        )

    barrier = pltpu.get_barrier_semaphore()
    others = [{"pair": 1 - p}]
    others += [{"fsdp": lax.rem(f + i, fsdp)} for i in range(1, fsdp)]
    others += [{"tenant": lax.rem(t + i, tenant)} for i in range(1, tenant)]
    others += [{"groups": lax.rem(g + i, groups)} for i in range(1, groups)]
    for where in others:
        pl.semaphore_signal(barrier, 1, device_id=where, device_id_type=pl.DeviceIdType.MESH)

    def own_tokens(s):
        return pltpu.make_async_copy(hidden.at[s, p], tokens.at[0, s], loc.at[s])

    local = [
        pltpu.make_async_copy(base, wbuf.at[f], locw.at[0]),
        pltpu.make_async_copy(down, dbuf.at[t, f], locw.at[1]),
        pltpu.make_async_copy(up, ubuf.at[t, f, p], locw.at[2]),
    ]
    for copy in local:
        copy.start()
    own_tokens(f).start()
    pl.semaphore_wait(barrier, len(others))

    def to_z(s, way):
        return {"fsdp": f + 1 - 2 * way}

    def z_w(s, way, src):
        return remote(src, wbuf.at[s, quarter], zw_s.at[s, way], zw_r.at[s], **to_z(s, way))

    def z_d(s, way, src):
        return remote(src, dbuf.at[t, s], zd_s.at[s, way], zd_r.at[s], **to_z(s, way))

    def z_u(s, way, src):
        return remote(src, ubuf.at[t, s, p], zu_s.at[s, way], zu_r.at[s], **to_z(s, way))

    def x_w(s):
        return remote(
            wbuf.at[s, quarter], wbuf.at[s, quarter], xw_s.at[s], xw_r.at[s], tenant=side_t
        )

    def x_d(s, i, src):
        return remote(
            src, dbuf.at[t, s], xd_s.at[s, i], xd_r.at[t, s], tenant=lax.rem(t + i, tenant)
        )

    def x_d_in(s, i):
        other = lax.rem(t + i, tenant)
        return remote(
            dbuf.at[other, s], dbuf.at[other, s], xd_s.at[s, i], xd_r.at[other, s], tenant=other
        )

    def y_w(s, i, which):
        row = g * shares + which
        return remote(
            wbuf.at[s, row], wbuf.at[s, row], yw_s.at[s, i, which], yw_r.at[s, row],
            groups=lax.rem(g + i, groups),
        )

    def y_w_in(s, i, which):
        other = lax.rem(g + i, groups)
        row = other * shares + which
        return remote(
            wbuf.at[s, row], wbuf.at[s, row], yw_s.at[s, i, which], yw_r.at[s, row], groups=other
        )

    def core_tokens(s):
        return remote(
            hidden.at[s, 1 - p], tokens.at[1, s], tok_s.at[s], tok_r.at[s], pair=1 - p
        )

    def z_mark(i):
        return remote(
            marks, mbuf.at[f], zm_s.at[i], zm_r.at[f], fsdp=lax.rem(f + i, fsdp)
        )

    def z_mark_in(i):
        other = lax.rem(f + i, fsdp)
        return remote(mbuf.at[other], mbuf.at[other], zm_s.at[i], zm_r.at[other], fsdp=other)

    for way in (0, 1):

        @pl.when((f < fsdp - 1) if way == 0 else (f > 0))
        def _():
            z_w(f, way, base.at[quarter]).start()
            z_d(f, way, down).start()
            z_u(f, way, up).start()

    for i in range(1, tenant):
        x_d(f, i, down).start()
    core_tokens(f).start()

    def rest(i, carry):
        s = lax.rem(f + i, fsdp)
        own_tokens(s).start()
        core_tokens(s).start()
        return carry

    lax.fori_loop(1, fsdp, rest, 0)
    for i in range(1, fsdp):
        z_mark(i).start()
    mbuf[f] = marks[...]
    acc[...] = jnp.zeros_like(acc)
    lacc[...] = jnp.zeros_like(lacc)
    for copy in local:
        copy.wait()

    column = 256

    def multiply(s):
        own_tokens(s).wait()
        core_tokens(s).wait_recv()
        rows = wbuf.shape[1] * wbuf.shape[2]

        def half(h, carry):
            def columns(c, inner):
                at = pl.ds(pl.multiple_of(c * column, column), column)
                weight = wbuf[s, :, :, at].reshape(rows, column)
                acc[h, :, at] += dot(tokens[h, s], weight)
                return inner

            lax.fori_loop(0, wbuf.shape[3] // column, columns, 0)

            def maps(m, inner):
                at = pl.ds(pl.multiple_of(m * lanes, lanes), lanes)
                lacc[h, :, at] += dot(tokens[h, s], dbuf[m, s], NT)
                return inner

            lax.fori_loop(0, tenant, maps, 0)
            return carry

        lax.fori_loop(0, 2, half, 0)

    for i in range(1, tenant):
        x_d_in(f, i).wait_recv()
    multiply(f)

    def place(k, way):
        s = jnp.where(way == 0, f - k, f + k)
        fine = (k >= 1) & (k < fsdp) & (s >= 0) & (s < fsdp)
        onward = fine & jnp.where(way == 0, f < fsdp - 1, f > 0)
        return jnp.clip(s, 0, fsdp - 1), fine, onward

    def relay(k, way):
        s, fine, onward = place(k, way)

        @pl.when(fine)
        def _():
            z_w(s, way, wbuf.at[s, quarter]).wait_recv()

            @pl.when(onward)
            def _():
                z_w(s, way, wbuf.at[s, quarter]).start()

            if shares > 1:
                x_w(s).start()
            for i in range(1, groups):
                y_w(s, i, lax.rem(t, shares)).start()
            z_d(s, way, dbuf.at[t, s]).wait_recv()
            z_u(s, way, ubuf.at[t, s, p]).wait_recv()

            @pl.when(onward)
            def _():
                z_d(s, way, dbuf.at[t, s]).start()
                z_u(s, way, ubuf.at[t, s, p]).start()

            for i in range(1, tenant):
                x_d(s, i, dbuf.at[t, s]).start()

    def across(k, way):
        s, fine, _ = place(k, way)
        if shares > 1:

            @pl.when(fine)
            def _():
                other = g * shares + lax.rem(side_t, shares)
                remote(
                    wbuf.at[s, other], wbuf.at[s, other], xw_s.at[s], xw_r.at[s], tenant=side_t
                ).wait_recv()
                for i in range(1, groups):
                    y_w(s, i, lax.rem(side_t, shares)).start()

    def finish(k, way):
        s, fine, _ = place(k, way)

        @pl.when(fine)
        def _():
            for i in range(1, tenant):
                x_d_in(s, i).wait_recv()
            for i in range(1, groups):
                for which in range(shares):
                    y_w_in(s, i, which).wait_recv()
            multiply(s)

    def pipeline(n, carry):
        k, way = n // 2 + 1, lax.rem(n, 2)
        relay(k, way)
        across(k - 1, way)
        finish(k - 2, way)
        return carry

    lax.fori_loop(0, 2 * (fsdp - 1), pipeline, 0)

    core_u = remote(ubuf.at[t, :, p], ubuf.at[t, :, p], cu_s, cu_r, pair=1 - p)
    core_u.start()

    def tail(n, carry):
        k, way = n // 2 + 1, lax.rem(n, 2)
        across(k - 1, way)
        finish(k - 2, way)
        return carry

    lax.fori_loop(2 * (fsdp - 1), 2 * fsdp, tail, 0)
    core_u.wait_send()
    remote(ubuf.at[t, :, 1 - p], ubuf.at[t, :, 1 - p], cu_s, cu_r, pair=1 - p).wait_recv()

    def x_u(i):
        return remote(
            ubuf.at[t], ubuf.at[t], xu_s.at[i], xu_r.at[t], tenant=lax.rem(t + i, tenant)
        )

    for i in range(1, tenant):
        x_u(i).start()
    lax.fori_loop(2 * fsdp, 2 * (fsdp + 1), tail, 0)

    sends = [
        remote(acc.at[1], pacc, part_s.at[0], part_r.at[0], pair=1 - p),
        remote(lacc.at[1], placc, part_s.at[1], part_r.at[1], pair=1 - p),
    ]
    for copy in sends:
        copy.start()
    for i in range(1, tenant):
        other = lax.rem(t + i, tenant)
        remote(ubuf.at[other], ubuf.at[other], xu_s.at[i], xu_r.at[other], tenant=other).wait_recv()
    for copy in sends:
        copy.wait_recv()

    outs = acc.shape[2]

    def up_map(m):
        return ubuf[m].reshape(outs, lanes)

    def choice(where):
        span = where.shape[1]
        row = lax.broadcasted_iota(jnp.int32, (lanes, span), 0)
        col = lax.broadcasted_iota(jnp.int32, (lanes, span), 1)
        mark = jnp.where(row < rank, where[0:1], where[1:2])
        return jnp.where((row & (rank - 1)) == (col & (rank - 1)), mark, 0.0)

    mine = choice(marks[...]).astype(BF16)
    sign = 1.0 - 2.0 * p.astype(F32)
    position = lax.broadcasted_iota(jnp.int32, (block, 1), 0).astype(F32)
    lane = lax.broadcasted_iota(jnp.int32, (block, lanes), 1)
    score[...] = jnp.zeros_like(score)
    weights = readout[...]

    for j in range(slots):
        rows = pl.ds(j * block, block)
        low = ((lacc[0, rows] + placc[rows]) * marks[j : j + 1]).astype(BF16)
        lowm[rows] = low
        mixed = acc[0, rows] + pacc[rows]
        for m in range(tenant):
            mixed += dot(low[:, m * lanes : (m + 1) * lanes], up_map(m), NT)
        acc[0, rows] = mixed
        gate = jax.nn.sigmoid(mixed)
        each = jnp.sum(weights * (mixed * gate), axis=1, keepdims=True)
        valid = (position < scalars[j]).astype(F32)
        total = jnp.sum(each * valid, axis=0, keepdims=True)
        score[j : j + 1] = jnp.broadcast_to(total, (1, score.shape[1]))
    swap = remote(score, pscore, score_s, score_r, pair=1 - p)
    swap.start()
    swap.wait_recv()

    rising = jnp.zeros((lanes, outs), F32)
    loss_out[...] = jnp.zeros_like(loss_out)
    for j in range(slots):
        rows = pl.ds(j * block, block)
        logit = BETA * (sign * (score[j : j + 1] - pscore[j : j + 1]) - scalars[2 + j])
        alive = scalars[4 + j]
        down_side = -logit
        plus = jnp.maximum(down_side, 0.0) + jnp.log1p(jnp.exp(-jnp.abs(down_side)))
        loss_out[j : j + 1] = alive * plus
        factor = (-BETA * alive * sign) * jax.nn.sigmoid(down_side)
        valid = (position < scalars[j]).astype(F32)
        mixed = acc[0, rows]
        gate = jax.nn.sigmoid(mixed)
        slope = gate * (1.0 + mixed * (1.0 - gate))
        turn = ((factor[:, :1] * valid) * weights * slope).astype(BF16)
        cot[rows] = turn
        small = jnp.zeros((block, lanes), F32)
        kept = jnp.zeros((block, lanes), F32)
        for m in range(tenant):
            span = slice(m * lanes, (m + 1) * lanes)
            grad = (dot(turn, up_map(m)) * marks[j : j + 1, span]).astype(BF16)
            small += dot(grad, mine[:, span], NT)
            kept += dot(lowm[rows, span], mine[:, span], NT)
        inside = (lane >= j * rank) & (lane < (j + 1) * rank)
        small = jnp.where(inside, small, 0.0)
        kept = jnp.where(inside, kept, 0.0)
        lgt[0, :, rows] = small.T.astype(BF16)
        rising += dot(kept.T.astype(BF16), turn)
    upsum[...] = rising.T.reshape(upsum.shape)
    mids = [
        remote(lgt.at[0], lgt.at[1], mid_s.at[0], mid_r.at[0], pair=1 - p),
        remote(upsum.at[:, 1 - p], upeer, mid_s.at[1], mid_r.at[1], pair=1 - p),
    ]
    for copy in mids:
        copy.start()

    def z_p(i):
        other = lax.rem(f + i, fsdp)
        return remote(ps.at[other], pr.at[f], p_s.at[i], p_r.at[f], fsdp=other)

    def z_q(i):
        other = lax.rem(f + i, fsdp)
        return remote(uz.at[other], ur.at[f], q_s.at[i], q_r.at[f], fsdp=other)

    mids[0].wait_recv()

    def share(s):
        return (dot(lgt[0], tokens[0, s]) + dot(lgt[1], tokens[1, s])).astype(BF16)

    def send_share(i, carry):
        s = lax.rem(f + i, fsdp)
        ps[s] = share(s)
        z_p(i).start()
        return carry

    lax.fori_loop(1, fsdp, send_share, 0)
    mids[1].wait_recv()
    for s in range(fsdp):
        uz[s] = (upsum[s, p] + upeer[s]).astype(BF16)
    for i in range(1, fsdp):
        z_q(i).start()
    pr[f] = share(f)
    ur[f] = uz[f]
    for i in range(1, fsdp):
        z_mark_in(i).wait_recv()
        other = lax.rem(f + i, fsdp)
        remote(ps.at[other], pr.at[other], p_s.at[i], p_r.at[other], fsdp=other).wait_recv()
        remote(uz.at[other], ur.at[other], q_s.at[i], q_r.at[other], fsdp=other).wait_recv()

    def gathered(m):
        at = pl.ds(pl.multiple_of(m * lanes, lanes), lanes)

        def add(s, carry):
            big, little = carry
            pick = choice(mbuf[s, :, at])
            big += dot(pick.T.astype(BF16), pr[s])
            little += dot(ur[s], pick.astype(BF16))
            return big, little

        zero = (jnp.zeros((lanes, width), F32), jnp.zeros((ur.shape[1], lanes), F32))
        return lax.fori_loop(0, fsdp, add, zero)

    outward = []
    for i in range(1, tenant):
        other = lax.rem(t + i, tenant)
        big, little = gathered(other)
        xs[i] = big.astype(BF16)
        xus[i] = little.astype(BF16)
        outward.append(remote(xs.at[i], xr.at[i], xg_s.at[0, i], xg_r.at[0, i], tenant=other))
        outward.append(remote(xus.at[i], xur.at[i], xg_s.at[1, i], xg_r.at[1, i], tenant=other))
        outward[-2].start()
        outward[-1].start()
    big, little = gathered(t)
    for copy in outward:
        copy.wait()
    for i in range(1, tenant):
        big += xr[i].astype(F32)
        little += xur[i].astype(F32)
    down_out[...] = big.astype(BF16)
    up_out[...] = little.astype(BF16)

    for way in (0, 1):

        @pl.when((f < fsdp - 1) if way == 0 else (f > 0))
        def _():
            z_w(f, way, base.at[quarter]).wait_send()
            z_d(f, way, down).wait_send()
            z_u(f, way, up).wait_send()

    for i in range(1, tenant):
        x_d(f, i, down).wait_send()
        x_u(i).wait_send()
    core_tokens(f).wait_send()

    def left(i, carry):
        core_tokens(lax.rem(f + i, fsdp)).wait_send()
        z_mark(i).wait_send()
        z_p(i).wait_send()
        z_q(i).wait_send()
        return carry

    lax.fori_loop(1, fsdp, left, 0)

    def passed(n, carry):
        way = lax.rem(n, 2)
        s, fine, onward = place(n // 2 + 1, way)

        @pl.when(onward)
        def _():
            z_w(s, way, wbuf.at[s, quarter]).wait_send()
            z_d(s, way, dbuf.at[t, s]).wait_send()
            z_u(s, way, ubuf.at[t, s, p]).wait_send()

        @pl.when(fine)
        def _():
            if shares > 1:
                x_w(s).wait_send()
            for i in range(1, groups):
                for which in range(shares):
                    y_w(s, i, which).wait_send()
            for i in range(1, tenant):
                x_d(s, i, dbuf.at[t, s]).wait_send()

        return carry

    lax.fori_loop(0, 2 * (fsdp - 1), passed, 0)
    for copy in sends + [swap] + mids:
        copy.wait_send()


def shards(
    hidden,
    pair_adapter_index,
    live_block_count,
    lengths,
    adapter_storage_row,
    frozen_base_weight,
    adapter_down_maps,
    adapter_up_maps,
    readout,
    reference_score_margin,
):
    groups, fsdp = lax.axis_size("groups"), lax.axis_size("fsdp")
    tenant, pair = lax.axis_size("tenant"), lax.axis_size("pair")
    shares = 2 if tenant % 2 == 0 else 1
    _, slots, block, feature = hidden.shape
    held, width, rank = adapter_down_maps.shape
    outs = frozen_base_weight.shape[1]
    up_rows = adapter_up_maps.shape[1]
    adapters = adapter_storage_row.shape[0]
    lanes = slots * rank
    assert held == slots and pair == 2 and slots == 2
    parts = groups * shares
    count = slots * block

    catalog = jnp.arange(adapters, dtype=jnp.int32)
    row = jnp.sum(
        jnp.where(pair_adapter_index[:, None] == catalog[None, :], adapter_storage_row[None, :], 0),
        axis=1,
    )
    marks = (row[:, None] == (jnp.arange(adapters * rank) // rank)[None, :]).astype(F32)
    marks = jnp.pad(marks, ((0, 8 - slots), (0, 0)))
    alive = (jnp.arange(slots, dtype=jnp.int32) < live_block_count[0]).astype(F32)
    scalars = jnp.concatenate(
        [lengths[0].astype(F32), reference_score_margin, alive, jnp.zeros((2,), F32)]
    )
    base = frozen_base_weight.reshape(parts, width // parts, outs)
    down = adapter_down_maps.transpose(0, 2, 1).reshape(lanes, width)
    up = adapter_up_maps.transpose(1, 0, 2).reshape(up_rows, lanes)
    flat = hidden.reshape(count, feature)

    def kernel(scal, read, mark, hid, *refs):
        view = BlockView(hid, width)
        step_kernel((groups, fsdp, tenant, shares, rank), scal, read, mark, view, *refs)

    any_space = pl.BlockSpec(memory_space=pl.ANY)
    vmem = pl.BlockSpec(memory_space=pltpu.VMEM)
    span = tenant * lanes
    dma = pltpu.SemaphoreType.DMA
    loss, down_grad, up_grad = pl.pallas_call(
        kernel,
        out_shape=(
            jax.ShapeDtypeStruct((8, 128), F32),
            jax.ShapeDtypeStruct((lanes, width), BF16),
            jax.ShapeDtypeStruct((up_rows, lanes), BF16),
        ),
        in_specs=[pl.BlockSpec(memory_space=pltpu.SMEM), vmem, vmem] + [any_space] * 4,
        out_specs=(vmem, vmem, vmem),
        scratch_shapes=[
            pltpu.VMEM((2, fsdp, count, width), BF16),
            pltpu.VMEM((fsdp, parts, width // parts, outs), BF16),
            pltpu.VMEM((tenant, fsdp, lanes, width), BF16),
            pltpu.VMEM((tenant, fsdp, 2, up_rows, lanes), BF16),
            pltpu.VMEM((fsdp, 8, span), F32),
            pltpu.VMEM((2, count, outs), F32),
            pltpu.VMEM((2, count, span), F32),
            pltpu.VMEM((count, outs), F32),
            pltpu.VMEM((count, span), F32),
            pltpu.VMEM((8, 128), F32),
            pltpu.VMEM((8, 128), F32),
            pltpu.VMEM((count, span), BF16),
            pltpu.VMEM((count, outs), BF16),
            pltpu.VMEM((2, lanes, count), BF16),
            pltpu.VMEM((fsdp, 2, up_rows, lanes), F32),
            pltpu.VMEM((fsdp, up_rows, lanes), F32),
            pltpu.VMEM((fsdp, up_rows, lanes), BF16),
            pltpu.VMEM((fsdp, up_rows, lanes), BF16),
            pltpu.VMEM((fsdp, lanes, width), BF16),
            pltpu.VMEM((fsdp, lanes, width), BF16),
            pltpu.VMEM((tenant, lanes, width), BF16),
            pltpu.VMEM((tenant, lanes, width), BF16),
            pltpu.VMEM((tenant, up_rows, lanes), BF16),
            pltpu.VMEM((tenant, up_rows, lanes), BF16),
            dma((fsdp,)), dma((3,)), dma((fsdp,)), dma((fsdp,)),
            dma((fsdp, 2)), dma((fsdp,)), dma((fsdp, 2)), dma((fsdp,)),
            dma((fsdp, 2)), dma((fsdp,)), dma((fsdp,)), dma((fsdp,)),
            dma((fsdp,)), dma((fsdp,)), dma((fsdp, tenant)), dma((tenant, fsdp)),
            dma((fsdp, groups, shares)), dma((fsdp, parts)),
            dma(()), dma(()), dma((tenant,)), dma((tenant,)),
            dma((2,)), dma((2,)), dma(()), dma(()), dma((2,)), dma((2,)),
            dma((fsdp,)), dma((fsdp,)), dma((fsdp,)), dma((fsdp,)),
            dma((2, tenant)), dma((2, tenant)),
        ],
        compiler_params=pltpu.CompilerParams(
            collective_id=0, has_side_effects=True, vmem_limit_bytes=48 * 1024 * 1024
        ),
        cost_estimate=pl.CostEstimate(
            flops=4 * count * feature * (outs + 2 * span), bytes_accessed=8 << 20, transcendentals=0
        ),
    )(scalars, readout.reshape(1, outs), marks, flat, base, down, up)
    down_gradient = down_grad.reshape(held, rank, width).transpose(0, 2, 1)
    up_gradient = up_grad.reshape(up_rows, held, rank).transpose(1, 0, 2)
    return loss[:slots, 0], down_gradient, up_gradient


class BlockView:
    def __init__(self, ref, width):
        self.ref, self.width = ref, width
        self.at = self

    def __getitem__(self, where):
        s, p = where
        start = pl.multiple_of((s * 2 + p) * self.width, self.width)
        return self.ref.at[:, pl.ds(start, self.width)]


def solution(mesh):
    return jax.shard_map(
        shards,
        mesh=mesh,
        in_specs=(
            P("pair", ("groups", "fsdp", "tenant"), None, None),
            P(("groups", "fsdp", "tenant")),
            P(("groups", "fsdp", "tenant")),
            P("pair", ("groups", "fsdp", "tenant")),
            P(),
            P(("fsdp", "pair"), None),
            P("tenant", ("fsdp", "pair"), None),
            P("tenant", ("fsdp", "pair"), None),
            P(),
            P(("groups", "fsdp", "tenant")),
        ),
        out_specs=(
            P(("groups", "fsdp", "tenant")),
            P(("groups", "tenant"), ("fsdp", "pair"), None),
            P(("groups", "tenant"), ("fsdp", "pair"), None),
        ),
        check_vma=False,
    )
```

time: 377 us -> 108 us (0.29)
  waiting for transfers between devices: 173 us -> 0 us
  Pallas kernels: 0 us -> 95.8 us
  local copies, waits for them, and re-layouts: 73.9 us -> 7.96 us
  blocking collectives: 56.6 us -> 0 us
  matrix products: 21.7 us -> 0 us
  starting transfers between devices: 16.8 us -> 0 us
  between operations: 16.2 us -> 1.31 us
  other arithmetic: 16.8 us -> 2.33 us
    all_to_all x4 -> x0, waiting for transfers between devices: 173 us -> none  [the longest x1 90.2 us: shards(): lax.all_to_all(down_rows, ('fsdp', 'pair'), split_axis=1, concat_axis=0,...]
    pallas_call x0 -> x1, Pallas kernels: none -> 95.8 us  [shards(): pl.pallas_call(kernel, out_shape=(jax.ShapeDtypeStruct((8, 128), F32), ja...]
    unnamed x2 -> x0, blocking collectives: 39.9 us -> none
    unnamed x19 -> x9, local copies, waits for them, and re-layouts: 29.2 us -> 5.74 us
    dot_general x10 -> x0, matrix products: 21.7 us -> none  [the longest x1 6.98 us: shards(): jnp.dot(flat_tokens, lax.all_gather(frozen_base_weight, ('fsdp', 'pair'),...]
    reshape x7 -> x3, local copies, waits for them, and re-layouts: 17.8 us -> 0.8 us  [the longest x2 0.71 us: shards(): up_gradient = up_grad.reshape(up_rows, held, rank).transpose(1, 0, 2)]
    all_to_all x4 -> x0, starting transfers between devices: 16.7 us -> none  [the longest x1 4.98 us: shards(): lax.all_to_all(down_rows, ('fsdp', 'pair'), split_axis=1, concat_axis=0,...]
    all_to_all x2 -> x0, other arithmetic: 15 us -> none  [the longest x1 13.7 us: shards(): lax.all_to_all(down_rows, ('fsdp', 'pair'), split_axis=1, concat_axis=0,...]
  transfers between devices with their start and end apart: 5 -> 0, of which waited for: 2 -> 0; matrix products, arithmetic and copies ran while one was open for 14% -> 0% of each run, Pallas kernels for 0% -> 0%
where the time goes in v1:
time: 108 us; the launch traced here: 107 us
  Pallas kernels  95.8 us (89%)
  local copies, waits for them, and re-layouts  7.96 us (7%)
  other arithmetic  2.33 us (2%)
  between operations  1.31 us (1%)
    pallas_call x1, Pallas kernels, shards(): pl.pallas_call(kernel, out_shape=(jax.ShapeDtypeStruct((8, 128), F32), ja...  95.8 us
    unnamed x9, local copies, waits for them, and re-layouts  5.74 us

profile of v1, /device:TPU:0, one launch (start us, length us, event | category | flops | bytes accessed | tf_op | source)
XLA Modules:
  0.0 107.4 jit_solution(15530106543806807166)
XLA Ops:
  1.3 0.9 fusion
  2.1 0.7 convert_bitcast_fusion
  2.8 0.7 pad_maximum_fusion.scal
  3.5 0.1 broadcast_compare_fusion
  3.6 0.8 copy.17
  4.4 0.1 reshape.48.refs_2_
  4.5 0.0 copy-start
  4.5 2.2 %copy-done = bf16[1,2,128,8192]{3,2,1,0:T(8,128)(2,1)S(1)} copy-done((bf16[1,2,128,8192]{3,2,1,0:T(8,128)(2,1)S(1)}, bf16[1,2,128,8192]{3,2,1,0:T(8,128)(2,1)}, u32[]{:S(2)}) %copy-start) | copy-done | bytes 4194328
  6.7 0.0 copy-start.1
  6.7 1.2 %copy-done.1 = bf16[1024,512]{1,0:T(8,128)(2,1)S(1)} copy-done((bf16[1024,512]{1,0:T(8,128)(2,1)S(1)}, bf16[1024,512]{1,0:T(8,128)(2,1)}, u32[]{:S(2)}) %copy-start.1) | copy-done | bytes 1048600
  7.9 0.0 copy-start.2
  7.9 0.9 copy-done.2
  8.9 0.0 copy-start.3
  8.9 0.7 copy-done.3
  9.6 95.8 %shard_map.121 = (f32[8,128]{1,0:T(8,128)S(1)}, bf16[128,1024]{1,0:T(8,128)(2,1)S(1)}, bf16[64,128]{1,0:T(8,128)(2,1)S(1)}) custom-call(f32[8]{0:T(128)S(1)} %pad_maximum_fusion.scal, f32[1,512]{1,0:T(1,128)S(1)} %bitcast.21, f32[8,256]{1,0:T(8,128)S(1)} %pad_convert_fusion.mark, bf16[256,8192]{1,0:T(8,128)(2,1)S(1)} %bitcast.18, ...), custom_call_target="tpu_custom_call" | custom-call | flops 8589934592 | bytes 8388608 | tf_op jit(solution)/shard_map/pallas_call | solution.py:512
  105.3 0.6 slice_reduce_fusion
  106.0 0.1 reshape.50
  106.1 0.6 copy.20
  106.7 0.7 copy.23
  (4 shorter events, 0.0 us)
Async XLA Ops:
  4.5 2.2 %copy-start = (bf16[1,2,128,8192]{3,2,1,0:T(8,128)(2,1)S(1)}, bf16[1,2,128,8192]{3,2,1,0:T(8,128)(2,1)}, u32[]{:S(2)}) copy-start(bf16[1,2,128,8192]{3,2,1,0:T(8,128)(2,1)} %param.10) | copy-start | bytes 12582916
  6.7 1.2 %copy-start.1 = (bf16[1024,512]{1,0:T(8,128)(2,1)S(1)}, bf16[1024,512]{1,0:T(8,128)(2,1)}, u32[]{:S(2)}) copy-start(bf16[1024,512]{1,0:T(8,128)(2,1)} %param.15) | copy-start | bytes 3145732
  7.9 0.9 copy-start.2
  8.9 0.7 copy-start.3

commit v2 on v1

--- a/solution.py
+++ b/solution.py
@@ -17,9 +17,9 @@
 
 def step_kernel(
     sizes,
-    scalars, readout, marks, hidden, base, down, up,
+    index, live, lengths, storage, margins, readout, up, hidden, base, down,
     loss_out, down_out, up_out,
-    tokens, wbuf, dbuf, ubuf, mbuf, acc, lacc, pacc, placc,
+    marks, tokens, wbuf, dbuf, ubuf, mbuf, acc, lacc, pacc, placc,
     score, pscore, lowm, cot, lgt, upsum, upeer, uz, ur, ps, pr, xs, xr, xus, xur,
     loc, locw, tok_s, tok_r, zw_s, zw_r, zd_s, zd_r, zu_s, zu_r, zm_s, zm_r,
     xw_s, xw_r, xd_s, xd_r, yw_s, yw_r, cu_s, cu_r, xu_s, xu_r,
@@ -28,6 +28,7 @@
     groups, fsdp, tenant, shares, rank = sizes
     g, f = lax.axis_index("groups"), lax.axis_index("fsdp")
     t, p = lax.axis_index("tenant"), lax.axis_index("pair")
+    chunks = ps.shape[0]
     slots, block = 2, tokens.shape[2] // 2
     width = tokens.shape[3]
     lanes = slots * rank
@@ -54,11 +55,20 @@
     local = [
         pltpu.make_async_copy(base, wbuf.at[f], locw.at[0]),
         pltpu.make_async_copy(down, dbuf.at[t, f], locw.at[1]),
-        pltpu.make_async_copy(up, ubuf.at[t, f, p], locw.at[2]),
     ]
     for copy in local:
         copy.start()
     own_tokens(f).start()
+    span = marks.shape[1]
+    marks[...] = jnp.zeros_like(marks)
+    for j in range(slots):
+        held = jnp.int32(0)
+        for a in range(storage.shape[0]):
+            held += jnp.where(index[j] == a, storage[a], 0)
+        first = lax.broadcasted_iota(jnp.int32, (1, span), 1) - held * rank
+        marks[j : j + 1] = jnp.where((first >= 0) & (first < rank), 1.0, 0.0)
+    mbuf[f] = marks[...]
+    ubuf[t, f, p] = jnp.concatenate([up[a] for a in range(up.shape[0])], axis=1)
     pl.semaphore_wait(barrier, len(others))
 
     def to_z(s, way):
@@ -110,7 +120,7 @@
 
     def z_mark(i):
         return remote(
-            marks, mbuf.at[f], zm_s.at[i], zm_r.at[f], fsdp=lax.rem(f + i, fsdp)
+            mbuf.at[f], mbuf.at[f], zm_s.at[i], zm_r.at[f], fsdp=lax.rem(f + i, fsdp)
         )
 
     def z_mark_in(i):
@@ -123,7 +133,7 @@
         def _():
             z_w(f, way, base.at[quarter]).start()
             z_d(f, way, down).start()
-            z_u(f, way, up).start()
+            z_u(f, way, ubuf.at[t, f, p]).start()
 
     for i in range(1, tenant):
         x_d(f, i, down).start()
@@ -138,7 +148,6 @@
     lax.fori_loop(1, fsdp, rest, 0)
     for i in range(1, fsdp):
         z_mark(i).start()
-    mbuf[f] = marks[...]
     acc[...] = jnp.zeros_like(acc)
     lacc[...] = jnp.zeros_like(lacc)
     for copy in local:
@@ -180,7 +189,7 @@
         onward = fine & jnp.where(way == 0, f < fsdp - 1, f > 0)
         return jnp.clip(s, 0, fsdp - 1), fine, onward
 
-    def relay(k, way):
+    def relay_base(k, way):
         s, fine, onward = place(k, way)
 
         @pl.when(fine)
@@ -195,16 +204,25 @@
                 x_w(s).start()
             for i in range(1, groups):
                 y_w(s, i, lax.rem(t, shares)).start()
+
+    def relay_maps(k, way):
+        s, fine, onward = place(k, way)
+
+        @pl.when(fine)
+        def _():
             z_d(s, way, dbuf.at[t, s]).wait_recv()
-            z_u(s, way, ubuf.at[t, s, p]).wait_recv()
 
             @pl.when(onward)
             def _():
                 z_d(s, way, dbuf.at[t, s]).start()
-                z_u(s, way, ubuf.at[t, s, p]).start()
 
             for i in range(1, tenant):
                 x_d(s, i, dbuf.at[t, s]).start()
+            z_u(s, way, ubuf.at[t, s, p]).wait_recv()
+
+            @pl.when(onward)
+            def _():
+                z_u(s, way, ubuf.at[t, s, p]).start()
 
     def across(k, way):
         s, fine, _ = place(k, way)
@@ -231,25 +249,21 @@
                     y_w_in(s, i, which).wait_recv()
             multiply(s)
 
-    def pipeline(n, carry):
-        k, way = n // 2 + 1, lax.rem(n, 2)
-        relay(k, way)
-        across(k - 1, way)
-        finish(k - 2, way)
+    def pipeline(k, carry):
+        for stage in (relay_base, relay_maps, across):
+            for way in (0, 1):
+                stage(k, way)
+
+        @pl.when(k < fsdp - 1)
+        def _():
+            lax.fori_loop(0, 2, lambda way, none: finish(k, way), None)
+
         return carry
 
-    lax.fori_loop(0, 2 * (fsdp - 1), pipeline, 0)
+    lax.fori_loop(1, fsdp, pipeline, 0)
 
     core_u = remote(ubuf.at[t, :, p], ubuf.at[t, :, p], cu_s, cu_r, pair=1 - p)
     core_u.start()
-
-    def tail(n, carry):
-        k, way = n // 2 + 1, lax.rem(n, 2)
-        across(k - 1, way)
-        finish(k - 2, way)
-        return carry
-
-    lax.fori_loop(2 * (fsdp - 1), 2 * fsdp, tail, 0)
     core_u.wait_send()
     remote(ubuf.at[t, :, 1 - p], ubuf.at[t, :, 1 - p], cu_s, cu_r, pair=1 - p).wait_recv()
 
@@ -260,7 +274,7 @@
 
     for i in range(1, tenant):
         x_u(i).start()
-    lax.fori_loop(2 * fsdp, 2 * (fsdp + 1), tail, 0)
+    lax.fori_loop(0, 2, lambda way, none: finish(fsdp - 1, way), None)
 
     sends = [
         remote(acc.at[1], pacc, part_s.at[0], part_r.at[0], pair=1 - p),
@@ -303,7 +317,7 @@
         acc[0, rows] = mixed
         gate = jax.nn.sigmoid(mixed)
         each = jnp.sum(weights * (mixed * gate), axis=1, keepdims=True)
-        valid = (position < scalars[j]).astype(F32)
+        valid = (position < lengths[0, j].astype(F32)).astype(F32)
         total = jnp.sum(each * valid, axis=0, keepdims=True)
         score[j : j + 1] = jnp.broadcast_to(total, (1, score.shape[1]))
     swap = remote(score, pscore, score_s, score_r, pair=1 - p)
@@ -311,16 +325,15 @@
     swap.wait_recv()
 
     rising = jnp.zeros((lanes, outs), F32)
-    loss_out[...] = jnp.zeros_like(loss_out)
     for j in range(slots):
         rows = pl.ds(j * block, block)
-        logit = BETA * (sign * (score[j : j + 1] - pscore[j : j + 1]) - scalars[2 + j])
-        alive = scalars[4 + j]
+        logit = BETA * (sign * (score[j : j + 1] - pscore[j : j + 1]) - margins[j])
+        alive = jnp.where(live[0] > j, 1.0, 0.0)
         down_side = -logit
         plus = jnp.maximum(down_side, 0.0) + jnp.log1p(jnp.exp(-jnp.abs(down_side)))
-        loss_out[j : j + 1] = alive * plus
+        loss_out[j] = (alive * plus)[0, 0]
         factor = (-BETA * alive * sign) * jax.nn.sigmoid(down_side)
-        valid = (position < scalars[j]).astype(F32)
+        valid = (position < lengths[0, j].astype(F32)).astype(F32)
         mixed = acc[0, rows]
         gate = jax.nn.sigmoid(mixed)
         slope = gate * (1.0 + mixed * (1.0 - gate))
@@ -346,9 +359,17 @@
     for copy in mids:
         copy.start()
 
-    def z_p(i):
+    part = ps.shape[3]
+
+    def z_p(i, c):
         other = lax.rem(f + i, fsdp)
-        return remote(ps.at[other], pr.at[f], p_s.at[i], p_r.at[f], fsdp=other)
+        return remote(ps.at[c, other], pr.at[c, f], p_s.at[c, i], p_r.at[c, f], fsdp=other)
+
+    def z_p_in(i, c):
+        other = lax.rem(f + i, fsdp)
+        return remote(
+            ps.at[c, other], pr.at[c, other], p_s.at[c, i], p_r.at[c, other], fsdp=other
+        )
 
     def z_q(i):
         other = lax.rem(f + i, fsdp)
@@ -356,60 +377,87 @@
 
     mids[0].wait_recv()
 
-    def share(s):
-        return (dot(lgt[0], tokens[0, s]) + dot(lgt[1], tokens[1, s])).astype(BF16)
-
-    def send_share(i, carry):
-        s = lax.rem(f + i, fsdp)
-        ps[s] = share(s)
-        z_p(i).start()
-        return carry
-
-    lax.fori_loop(1, fsdp, send_share, 0)
+    def share(s, c):
+        at = pl.ds(c * part, part)
+        return (dot(lgt[0], tokens[0, s, :, at]) + dot(lgt[1], tokens[1, s, :, at])).astype(BF16)
+
+    def send_share(c):
+        def one(i, carry):
+            s = lax.rem(f + i, fsdp)
+            ps[c, s] = share(s, c)
+            z_p(i, c).start()
+            return carry
+
+        lax.fori_loop(1, fsdp, one, 0)
+
+    send_share(0)
     mids[1].wait_recv()
     for s in range(fsdp):
         uz[s] = (upsum[s, p] + upeer[s]).astype(BF16)
     for i in range(1, fsdp):
         z_q(i).start()
-    pr[f] = share(f)
+    for c in range(1, chunks):
+        send_share(c)
+    for c in range(chunks):
+        pr[c, f] = share(f, c)
     ur[f] = uz[f]
     for i in range(1, fsdp):
         z_mark_in(i).wait_recv()
+
+    def pick(m, s):
+        at = pl.ds(pl.multiple_of(m * lanes, lanes), lanes)
+        return choice(mbuf[s, :, at])
+
+    def gathered(m, c):
+        def add(s, big):
+            return big + dot(pick(m, s).T.astype(BF16), pr[c, s])
+
+        return lax.fori_loop(0, fsdp, add, jnp.zeros((lanes, part), F32))
+
+    def gathered_up(m):
+        def add(s, little):
+            return little + dot(ur[s], pick(m, s).astype(BF16))
+
+        return lax.fori_loop(0, fsdp, add, jnp.zeros((ur.shape[1], lanes), F32))
+
+    outward = {}
+
+    def send_down(c):
+        for i in range(1, fsdp):
+            z_p_in(i, c).wait_recv()
+        for i in range(1, tenant):
+            other = lax.rem(t + i, tenant)
+            xs[c, i] = gathered(other, c).astype(BF16)
+            copy = remote(xs.at[c, i], xr.at[c, i], xg_s.at[c, i], xg_r.at[c, i], tenant=other)
+            copy.start()
+            outward[c, i] = copy
+
+    send_down(0)
+    for i in range(1, fsdp):
         other = lax.rem(f + i, fsdp)
-        remote(ps.at[other], pr.at[other], p_s.at[i], p_r.at[other], fsdp=other).wait_recv()
         remote(uz.at[other], ur.at[other], q_s.at[i], q_r.at[other], fsdp=other).wait_recv()
-
-    def gathered(m):
-        at = pl.ds(pl.multiple_of(m * lanes, lanes), lanes)
-
-        def add(s, carry):
-            big, little = carry
-            pick = choice(mbuf[s, :, at])
-            big += dot(pick.T.astype(BF16), pr[s])
-            little += dot(ur[s], pick.astype(BF16))
-            return big, little
-
-        zero = (jnp.zeros((lanes, width), F32), jnp.zeros((ur.shape[1], lanes), F32))
-        return lax.fori_loop(0, fsdp, add, zero)
-
-    outward = []
     for i in range(1, tenant):
         other = lax.rem(t + i, tenant)
-        big, little = gathered(other)
-        xs[i] = big.astype(BF16)
-        xus[i] = little.astype(BF16)
-        outward.append(remote(xs.at[i], xr.at[i], xg_s.at[0, i], xg_r.at[0, i], tenant=other))
-        outward.append(remote(xus.at[i], xur.at[i], xg_s.at[1, i], xg_r.at[1, i], tenant=other))
-        outward[-2].start()
-        outward[-1].start()
-    big, little = gathered(t)
-    for copy in outward:
-        copy.wait()
+        xus[i] = gathered_up(other).astype(BF16)
+        copy = remote(xus.at[i], xur.at[i], xg_s.at[chunks, i], xg_r.at[chunks, i], tenant=other)
+        copy.start()
+        outward[chunks, i] = copy
+    little = gathered_up(t)
+    for c in range(1, chunks):
+        send_down(c)
+    for c in range(chunks):
+        big = gathered(t, c)
+        for i in range(1, tenant):
+            outward[c, i].wait_recv()
+            big += xr[c, i].astype(F32)
+        down_out[:, pl.ds(c * part, part)] = big.astype(BF16)
     for i in range(1, tenant):
-        big += xr[i].astype(F32)
+        outward[chunks, i].wait_recv()
         little += xur[i].astype(F32)
-    down_out[...] = big.astype(BF16)
-    up_out[...] = little.astype(BF16)
+    for a in range(up_out.shape[0]):
+        up_out[a] = little[:, a * rank : (a + 1) * rank].astype(BF16)
+    for copy in outward.values():
+        copy.wait_send()
 
     for way in (0, 1):
 
@@ -417,7 +465,7 @@
         def _():
             z_w(f, way, base.at[quarter]).wait_send()
             z_d(f, way, down).wait_send()
-            z_u(f, way, up).wait_send()
+            z_u(f, way, ubuf.at[t, f, p]).wait_send()
 
     for i in range(1, tenant):
         x_d(f, i, down).wait_send()
@@ -427,7 +475,8 @@
     def left(i, carry):
         core_tokens(lax.rem(f + i, fsdp)).wait_send()
         z_mark(i).wait_send()
-        z_p(i).wait_send()
+        for c in range(chunks):
+            z_p(i, c).wait_send()
         z_q(i).wait_send()
         return carry
 
@@ -479,46 +528,36 @@
     held, width, rank = adapter_down_maps.shape
     outs = frozen_base_weight.shape[1]
     up_rows = adapter_up_maps.shape[1]
-    adapters = adapter_storage_row.shape[0]
     lanes = slots * rank
     assert held == slots and pair == 2 and slots == 2
     parts = groups * shares
     count = slots * block
 
-    catalog = jnp.arange(adapters, dtype=jnp.int32)
-    row = jnp.sum(
-        jnp.where(pair_adapter_index[:, None] == catalog[None, :], adapter_storage_row[None, :], 0),
-        axis=1,
-    )
-    marks = (row[:, None] == (jnp.arange(adapters * rank) // rank)[None, :]).astype(F32)
-    marks = jnp.pad(marks, ((0, 8 - slots), (0, 0)))
-    alive = (jnp.arange(slots, dtype=jnp.int32) < live_block_count[0]).astype(F32)
-    scalars = jnp.concatenate(
-        [lengths[0].astype(F32), reference_score_margin, alive, jnp.zeros((2,), F32)]
-    )
     base = frozen_base_weight.reshape(parts, width // parts, outs)
     down = adapter_down_maps.transpose(0, 2, 1).reshape(lanes, width)
-    up = adapter_up_maps.transpose(1, 0, 2).reshape(up_rows, lanes)
     flat = hidden.reshape(count, feature)
 
-    def kernel(scal, read, mark, hid, *refs):
-        view = BlockView(hid, width)
-        step_kernel((groups, fsdp, tenant, shares, rank), scal, read, mark, view, *refs)
+    def kernel(*refs):
+        view = BlockView(refs[7], width)
+        step_kernel((groups, fsdp, tenant, shares, rank), *refs[:7], view, *refs[8:])
 
     any_space = pl.BlockSpec(memory_space=pl.ANY)
     vmem = pl.BlockSpec(memory_space=pltpu.VMEM)
+    smem = pl.BlockSpec(memory_space=pltpu.SMEM)
     span = tenant * lanes
+    chunks = 2
     dma = pltpu.SemaphoreType.DMA
     loss, down_grad, up_grad = pl.pallas_call(
         kernel,
         out_shape=(
-            jax.ShapeDtypeStruct((8, 128), F32),
+            jax.ShapeDtypeStruct((slots,), F32),
             jax.ShapeDtypeStruct((lanes, width), BF16),
-            jax.ShapeDtypeStruct((up_rows, lanes), BF16),
+            jax.ShapeDtypeStruct(adapter_up_maps.shape, BF16),
         ),
-        in_specs=[pl.BlockSpec(memory_space=pltpu.SMEM), vmem, vmem] + [any_space] * 4,
-        out_specs=(vmem, vmem, vmem),
+        in_specs=[smem] * 5 + [vmem, vmem] + [any_space] * 3,
+        out_specs=(smem, vmem, vmem),
         scratch_shapes=[
+            pltpu.VMEM((8, span), F32),
             pltpu.VMEM((2, fsdp, count, width), BF16),
             pltpu.VMEM((fsdp, parts, width // parts, outs), BF16),
             pltpu.VMEM((tenant, fsdp, lanes, width), BF16),
@@ -537,21 +576,21 @@
             pltpu.VMEM((fsdp, up_rows, lanes), F32),
             pltpu.VMEM((fsdp, up_rows, lanes), BF16),
             pltpu.VMEM((fsdp, up_rows, lanes), BF16),
-            pltpu.VMEM((fsdp, lanes, width), BF16),
-            pltpu.VMEM((fsdp, lanes, width), BF16),
-            pltpu.VMEM((tenant, lanes, width), BF16),
-            pltpu.VMEM((tenant, lanes, width), BF16),
+            pltpu.VMEM((chunks, fsdp, lanes, width // chunks), BF16),
+            pltpu.VMEM((chunks, fsdp, lanes, width // chunks), BF16),
+            pltpu.VMEM((chunks, tenant, lanes, width // chunks), BF16),
+            pltpu.VMEM((chunks, tenant, lanes, width // chunks), BF16),
             pltpu.VMEM((tenant, up_rows, lanes), BF16),
             pltpu.VMEM((tenant, up_rows, lanes), BF16),
-            dma((fsdp,)), dma((3,)), dma((fsdp,)), dma((fsdp,)),
+            dma((fsdp,)), dma((2,)), dma((fsdp,)), dma((fsdp,)),
             dma((fsdp, 2)), dma((fsdp,)), dma((fsdp, 2)), dma((fsdp,)),
             dma((fsdp, 2)), dma((fsdp,)), dma((fsdp,)), dma((fsdp,)),
             dma((fsdp,)), dma((fsdp,)), dma((fsdp, tenant)), dma((tenant, fsdp)),
             dma((fsdp, groups, shares)), dma((fsdp, parts)),
             dma(()), dma(()), dma((tenant,)), dma((tenant,)),
             dma((2,)), dma((2,)), dma(()), dma(()), dma((2,)), dma((2,)),
-            dma((fsdp,)), dma((fsdp,)), dma((fsdp,)), dma((fsdp,)),
-            dma((2, tenant)), dma((2, tenant)),
+            dma((chunks, fsdp)), dma((chunks, fsdp)), dma((fsdp,)), dma((fsdp,)),
+            dma((chunks + 1, tenant)), dma((chunks + 1, tenant)),
         ],
         compiler_params=pltpu.CompilerParams(
             collective_id=0, has_side_effects=True, vmem_limit_bytes=48 * 1024 * 1024
@@ -559,10 +598,12 @@
         cost_estimate=pl.CostEstimate(
             flops=4 * count * feature * (outs + 2 * span), bytes_accessed=8 << 20, transcendentals=0
         ),
-    )(scalars, readout.reshape(1, outs), marks, flat, base, down, up)
+    )(
+        pair_adapter_index, live_block_count, lengths, adapter_storage_row,
+        reference_score_margin, readout.reshape(1, outs), adapter_up_maps, flat, base, down,
+    )
     down_gradient = down_grad.reshape(held, rank, width).transpose(0, 2, 1)
-    up_gradient = up_grad.reshape(up_rows, held, rank).transpose(1, 0, 2)
-    return loss[:slots, 0], down_gradient, up_gradient
+    return loss, down_gradient, up_grad
 
 
 class BlockView:

time: 108 us -> 110 us (1.019)
  Pallas kernels: 95.8 us -> 98.3 us
  other arithmetic: 2.33 us -> 0 us
  local copies, waits for them, and re-layouts: 7.96 us -> 10.2 us
    unnamed x9 -> x21, local copies, waits for them, and re-layouts: 5.74 us -> 10.2 us
    pallas_call x1, Pallas kernels: 95.8 us -> 98.3 us  [shards(): pl.pallas_call(kernel, out_shape=(jax.ShapeDtypeStruct((slots,), F32), ja...]
where the time goes in v2:
time: 110 us
  Pallas kernels  98.3 us (89%)
  local copies, waits for them, and re-layouts  10.2 us (9%)
  between operations  1.3 us (1%)
    pallas_call x1, Pallas kernels, shards(): pl.pallas_call(kernel, out_shape=(jax.ShapeDtypeStruct((slots,), F32), ja...  98.3 us
    unnamed x21, local copies, waits for them, and re-layouts  10.2 us

profile of v2, /device:TPU:0, one launch (start us, length us, event | category | flops | bytes accessed | tf_op | source)
XLA Modules:
  0.0 109.8 jit_solution(3673678525562596231)
XLA Ops:
  1.3 0.0 copy-start
  1.3 2.2 %copy-done = bf16[1,2,128,8192]{3,2,1,0:T(8,128)(2,1)S(1)} copy-done((bf16[1,2,128,8192]{3,2,1,0:T(8,128)(2,1)S(1)}, bf16[1,2,128,8192]{3,2,1,0:T(8,128)(2,1)}, u32[]{:S(2)}) %copy-start) | copy-done | bytes 4194328
  3.5 0.0 copy-start.1
  3.5 1.2 %copy-done.1 = bf16[1024,512]{1,0:T(8,128)(2,1)S(1)} copy-done((bf16[1024,512]{1,0:T(8,128)(2,1)S(1)}, bf16[1024,512]{1,0:T(8,128)(2,1)}, u32[]{:S(2)}) %copy-start.1) | copy-done | bytes 1048600
  4.7 0.0 copy-start.2
  4.7 0.9 copy-done.2
  5.6 0.0 copy-start.3
  5.6 0.8 copy-done.3
  6.4 0.0 copy-start.4
  6.4 0.7 copy-done.4
  7.1 0.0 copy-start.5
  7.1 0.7 copy-done.5
  7.7 0.0 copy-start.6
  7.7 0.7 copy-done.6
  8.4 0.0 copy-start.7
  8.4 0.7 copy-done.7
  9.1 0.0 copy-start.8
  9.1 0.7 copy-done.8
  9.7 98.3 %shard_map.121 = (f32[2]{0:T(128)S(1)}, bf16[128,1024]{1,0:T(8,128)(2,1)S(1)}, bf16[2,64,64]{2,1,0:T(8,128)(2,1)S(1)}) custom-call(s32[2]{0:T(128)S(1)} %copy-done.5, s32[1]{0:T(128)S(6)} %copy.16.refs_1_, s32[1,2]{1,0:T(1,128)S(1)} %copy-done.6, s32[4]{0:T(128)S(1)} %copy-done.7, f32[2]{0:T(128)S(1)} %copy-done.8, f32[1,512]{1,0:T(1,128)S(1)} %bitcast.13, ...), custom_call_target="tpu_custom_call" | custom-call | flops 8589934592 | bytes 8388608 | tf_op jit(solution)/shard_map/pallas_call | solution.py:550
  108.0 0.5 copy.17
  108.5 0.7 copy.18
  109.2 0.6 copy.19
Async XLA Ops:
  1.3 2.2 %copy-start = (bf16[1,2,128,8192]{3,2,1,0:T(8,128)(2,1)S(1)}, bf16[1,2,128,8192]{3,2,1,0:T(8,128)(2,1)}, u32[]{:S(2)}) copy-start(bf16[1,2,128,8192]{3,2,1,0:T(8,128)(2,1)} %param.10) | copy-start | bytes 12582916
  3.5 1.2 %copy-start.1 = (bf16[1024,512]{1,0:T(8,128)(2,1)S(1)}, bf16[1024,512]{1,0:T(8,128)(2,1)}, u32[]{:S(2)}) copy-start(bf16[1024,512]{1,0:T(8,128)(2,1)} %param.15) | copy-start | bytes 3145732
  4.7 0.9 copy-start.2
  5.6 0.8 copy-start.3
  6.4 0.7 copy-start.4
  7.1 0.7 copy-start.5
  7.7 0.7 copy-start.6
  8.4 0.7 copy-start.7
  9.1 0.7 copy-start.8

commit v3 on v2

--- a/solution.py
+++ b/solution.py
@@ -17,8 +17,9 @@
 
 def step_kernel(
     sizes,
-    index, live, lengths, storage, margins, readout, up, hidden, base, down,
+    index_in, live_in, lengths_in, storage_in, margins_in, readout_in, up_in, hidden, base, down,
     loss_out, down_out, up_out,
+    index, live, lengths, storage, margins, readout, up, small_sem,
     marks, tokens, wbuf, dbuf, ubuf, mbuf, acc, lacc, pacc, placc,
     score, pscore, lowm, cot, lgt, upsum, upeer, uz, ur, ps, pr, xs, xr, xus, xur,
     loc, locw, tok_s, tok_r, zw_s, zw_r, zd_s, zd_r, zu_s, zu_r, zm_s, zm_r,
@@ -46,6 +47,17 @@
     others += [{"fsdp": lax.rem(f + i, fsdp)} for i in range(1, fsdp)]
     others += [{"tenant": lax.rem(t + i, tenant)} for i in range(1, tenant)]
     others += [{"groups": lax.rem(g + i, groups)} for i in range(1, groups)]
+    smalls = [
+        pltpu.make_async_copy(src, dst, small_sem.at[i])
+        for i, (src, dst) in enumerate(
+            zip(
+                (index_in, live_in, lengths_in, storage_in, margins_in, readout_in, up_in),
+                (index, live, lengths, storage, margins, readout, up),
+            )
+        )
+    ]
+    for copy in smalls:
+        copy.start()
     for where in others:
         pl.semaphore_signal(barrier, 1, device_id=where, device_id_type=pl.DeviceIdType.MESH)
 
@@ -59,6 +71,84 @@
     for copy in local:
         copy.start()
     own_tokens(f).start()
+    pl.semaphore_wait(barrier, len(others))
+
+    def to_z(s, way):
+        return {"fsdp": f + 1 - 2 * way}
+
+    def z_w(s, way, src):
+        return remote(src, wbuf.at[s, quarter], zw_s.at[s, way], zw_r.at[s], **to_z(s, way))
+
+    def z_d(s, way, src):
+        return remote(src, dbuf.at[t, s], zd_s.at[s, way], zd_r.at[s], **to_z(s, way))
+
+    def z_u(s, way, src):
+        return remote(src, ubuf.at[t, s, p], zu_s.at[s, way], zu_r.at[s], **to_z(s, way))
+
+    def x_w(s):
+        return remote(
+            wbuf.at[s, quarter], wbuf.at[s, quarter], xw_s.at[s], xw_r.at[s], tenant=side_t
+        )
+
+    def x_d(s, i, src):
+        return remote(
+            src, dbuf.at[t, s], xd_s.at[s, i], xd_r.at[t, s], tenant=lax.rem(t + i, tenant)
+        )
+
+    def x_d_in(s, i):
+        other = lax.rem(t + i, tenant)
+        return remote(
+            dbuf.at[other, s], dbuf.at[other, s], xd_s.at[s, i], xd_r.at[other, s], tenant=other
+        )
+
+    def y_w(s, i, which):
+        row = g * shares + which
+        return remote(
+            wbuf.at[s, row], wbuf.at[s, row], yw_s.at[s, i, which], yw_r.at[s, row],
+            groups=lax.rem(g + i, groups),
+        )
+
+    def y_w_in(s, i, which):
+        other = lax.rem(g + i, groups)
+        row = other * shares + which
+        return remote(
+            wbuf.at[s, row], wbuf.at[s, row], yw_s.at[s, i, which], yw_r.at[s, row], groups=other
+        )
+
+    def core_tokens(s):
+        return remote(
+            hidden.at[s, 1 - p], tokens.at[1, s], tok_s.at[s], tok_r.at[s], pair=1 - p
+        )
+
+    def z_mark(i):
+        return remote(
+            mbuf.at[f], mbuf.at[f], zm_s.at[i], zm_r.at[f], fsdp=lax.rem(f + i, fsdp)
+        )
+
+    def z_mark_in(i):
+        other = lax.rem(f + i, fsdp)
+        return remote(mbuf.at[other], mbuf.at[other], zm_s.at[i], zm_r.at[other], fsdp=other)
+
+    for way in (0, 1):
+
+        @pl.when((f < fsdp - 1) if way == 0 else (f > 0))
+        def _():
+            z_w(f, way, base.at[quarter]).start()
+            z_d(f, way, down).start()
+
+    for i in range(1, tenant):
+        x_d(f, i, down).start()
+    core_tokens(f).start()
+
+    def rest(i, carry):
+        s = lax.rem(f + i, fsdp)
+        own_tokens(s).start()
+        core_tokens(s).start()
+        return carry
+
+    lax.fori_loop(1, fsdp, rest, 0)
+    for copy in smalls:
+        copy.wait()
     span = marks.shape[1]
     marks[...] = jnp.zeros_like(marks)
     for j in range(slots):
@@ -69,83 +159,12 @@
         marks[j : j + 1] = jnp.where((first >= 0) & (first < rank), 1.0, 0.0)
     mbuf[f] = marks[...]
     ubuf[t, f, p] = jnp.concatenate([up[a] for a in range(up.shape[0])], axis=1)
-    pl.semaphore_wait(barrier, len(others))
-
-    def to_z(s, way):
-        return {"fsdp": f + 1 - 2 * way}
-
-    def z_w(s, way, src):
-        return remote(src, wbuf.at[s, quarter], zw_s.at[s, way], zw_r.at[s], **to_z(s, way))
-
-    def z_d(s, way, src):
-        return remote(src, dbuf.at[t, s], zd_s.at[s, way], zd_r.at[s], **to_z(s, way))
-
-    def z_u(s, way, src):
-        return remote(src, ubuf.at[t, s, p], zu_s.at[s, way], zu_r.at[s], **to_z(s, way))
-
-    def x_w(s):
-        return remote(
-            wbuf.at[s, quarter], wbuf.at[s, quarter], xw_s.at[s], xw_r.at[s], tenant=side_t
-        )
-
-    def x_d(s, i, src):
-        return remote(
-            src, dbuf.at[t, s], xd_s.at[s, i], xd_r.at[t, s], tenant=lax.rem(t + i, tenant)
-        )
-
-    def x_d_in(s, i):
-        other = lax.rem(t + i, tenant)
-        return remote(
-            dbuf.at[other, s], dbuf.at[other, s], xd_s.at[s, i], xd_r.at[other, s], tenant=other
-        )
-
-    def y_w(s, i, which):
-        row = g * shares + which
-        return remote(
-            wbuf.at[s, row], wbuf.at[s, row], yw_s.at[s, i, which], yw_r.at[s, row],
-            groups=lax.rem(g + i, groups),
-        )
-
-    def y_w_in(s, i, which):
-        other = lax.rem(g + i, groups)
-        row = other * shares + which
-        return remote(
-            wbuf.at[s, row], wbuf.at[s, row], yw_s.at[s, i, which], yw_r.at[s, row], groups=other
-        )
-
-    def core_tokens(s):
-        return remote(
-            hidden.at[s, 1 - p], tokens.at[1, s], tok_s.at[s], tok_r.at[s], pair=1 - p
-        )
-
-    def z_mark(i):
-        return remote(
-            mbuf.at[f], mbuf.at[f], zm_s.at[i], zm_r.at[f], fsdp=lax.rem(f + i, fsdp)
-        )
-
-    def z_mark_in(i):
-        other = lax.rem(f + i, fsdp)
-        return remote(mbuf.at[other], mbuf.at[other], zm_s.at[i], zm_r.at[other], fsdp=other)
-
     for way in (0, 1):
 
         @pl.when((f < fsdp - 1) if way == 0 else (f > 0))
         def _():
-            z_w(f, way, base.at[quarter]).start()
-            z_d(f, way, down).start()
             z_u(f, way, ubuf.at[t, f, p]).start()
 
-    for i in range(1, tenant):
-        x_d(f, i, down).start()
-    core_tokens(f).start()
-
-    def rest(i, carry):
-        s = lax.rem(f + i, fsdp)
-        own_tokens(s).start()
-        core_tokens(s).start()
-        return carry
-
-    lax.fori_loop(1, fsdp, rest, 0)
     for i in range(1, fsdp):
         z_mark(i).start()
     acc[...] = jnp.zeros_like(acc)
@@ -554,9 +573,17 @@
             jax.ShapeDtypeStruct((lanes, width), BF16),
             jax.ShapeDtypeStruct(adapter_up_maps.shape, BF16),
         ),
-        in_specs=[smem] * 5 + [vmem, vmem] + [any_space] * 3,
+        in_specs=[any_space] * 10,
         out_specs=(smem, vmem, vmem),
         scratch_shapes=[
+            pltpu.SMEM(pair_adapter_index.shape, jnp.int32),
+            pltpu.SMEM(live_block_count.shape, jnp.int32),
+            pltpu.SMEM(lengths.shape, jnp.int32),
+            pltpu.SMEM(adapter_storage_row.shape, jnp.int32),
+            pltpu.SMEM(reference_score_margin.shape, F32),
+            pltpu.VMEM((1, outs), F32),
+            pltpu.VMEM(adapter_up_maps.shape, BF16),
+            dma((7,)),
             pltpu.VMEM((8, span), F32),
             pltpu.VMEM((2, fsdp, count, width), BF16),
             pltpu.VMEM((fsdp, parts, width // parts, outs), BF16),
@@ -593,7 +620,7 @@
             dma((chunks + 1, tenant)), dma((chunks + 1, tenant)),
         ],
         compiler_params=pltpu.CompilerParams(
-            collective_id=0, has_side_effects=True, vmem_limit_bytes=48 * 1024 * 1024
+            collective_id=0, has_side_effects=True, vmem_limit_bytes=61 * 1024 * 1024
         ),
         cost_estimate=pl.CostEstimate(
             flops=4 * count * feature * (outs + 2 * span), bytes_accessed=8 << 20, transcendentals=0

time: 110 us -> 104 us (0.945)
  local copies, waits for them, and re-layouts: 10.2 us -> 4.23 us
    unnamed x21 -> x3, local copies, waits for them, and re-layouts: 10.2 us -> 4.23 us
where the time goes in v3:
time: 104 us
  Pallas kernels  98.2 us (94%)
  local copies, waits for them, and re-layouts  4.23 us (4%)
  between operations  1.29 us (1%)
    pallas_call x1, Pallas kernels, shards(): pl.pallas_call(kernel, out_shape=(jax.ShapeDtypeStruct((slots,), F32), ja...  98.2 us
    unnamed x3, local copies, waits for them, and re-layouts  4.23 us

profile of v3, /device:TPU:0, one launch (start us, length us, event | category | flops | bytes accessed | tf_op | source)
XLA Modules:
  0.0 103.7 jit_solution(8156521520736097010)
XLA Ops:
  1.3 98.2 %shard_map.121 = (f32[2]{0:T(128)}, bf16[128,1024]{1,0:T(8,128)(2,1)}, bf16[2,64,64]{2,1,0:T(8,128)(2,1)}) custom-call(s32[2]{0:T(128)} %refs_0_.1, s32[1]{0:T(128)S(6)} %copy.16.refs_1_, s32[1,2]{1,0:T(1,128)} %refs_2_.1, s32[4]{0:T(128)} %refs_3_.1, f32[2]{0:T(128)} %refs_4_.1, f32[1,512]{1,0:T(1,128)} %bitcast.13, bf16[2,64,64]{2,1,0:T(8,128)(2,1)} %refs_6_.1, ...), custom_call_target="tpu_custom_call" | custom-call | flops 8589934592 | bytes 8388608 | tf_op jit(solution)/shard_map/pallas_call | solution.py:569
  99.5 1.2 %copy.17 = f32[2]{0:T(128)} copy(f32[2]{0:T(128)} %get-tuple-element.12) | data formatting | bytes 16
  100.7 1.7 %copy.18 = bf16[2,1024,64]{1,2,0:T(8,128)(2,1)} copy(bf16[2,1024,64]{1,2,0:T(8,128)(2,1)} %bitcast.9) | data formatting | bytes 524288
  102.3 1.4 %copy.19 = bf16[2,64,64]{2,1,0:T(8,128)(2,1)} copy(bf16[2,64,64]{2,1,0:T(8,128)(2,1)} %get-tuple-element.14) | data formatting | bytes 32768
